TPU v7x, 512 devices: a whole 4x4x16 slice. The times are simulated.
512 devices in a mesh: section: 32 (over y, z_lo, core), blk: 16 (over z_hi, x).
Axes of the slice: x: 4, y: 4, z: 16 (z_hi: 4, z_lo: 4; z = z_hi * 4 + z_lo), core: 2. Of those that a mesh axis runs over, the one named last changes fastest.
Arguments:
- sent_grad: bfloat16 [32, 2048, 3072], P('section', 'blk'), may hold values from -6 to 6
- gates: bfloat16 [32, 2048, 2], P('section', 'blk'), may hold values from 0.049804688 to 0.94921875
- slot_token: int32 [32, 256], P('section'), may hold values from 0 to 2048, as said below
- slot_rank: int32 [32, 256], P('section'), may hold values from 0 to 1
- pre_act: bfloat16 [32, 256, 2, 8192], P('section', None, None, 'blk'), may hold values from -6 to 6
- down_weight: bfloat16 [32, 8192, 3072], P('section', 'blk'), may hold values from -0.0625 to 0.0625
Outputs:
- d_pre: bfloat16 [32, 256, 2, 8192], P('section', None, None, 'blk')
- d_gate: float32 [32, 256], P('section')
Inputs may be any that keep to these rules, and one draw needn't show every extreme that they name: `slot_token`: in every section the live slots come first and hold distinct tokens in ascending order; every later slot holds the pad value 2048. At most 32 slots of a section name tokens k * 128 to (k + 1) * 128 - 1 for any k, and in every section some k reaches that bound.
All inputs are finite; a program needn't handle non-finite values.
Results may differ from a plain program's by a relative error of at most 0.0029.
Values may be sent and summed in bfloat16 or wider, within the bound.
A program may use at most 64 MiB of HBM per device.

v0:
```python
import jax
import jax.numpy as jnp
from jax import lax
from jax.sharding import PartitionSpec as P


def shifted(value, axis, steps):
    count = lax.axis_size(axis)
    pairs = [(source, (source + steps) % count) for source in range(count)]
    return lax.ppermute(value, axis, pairs)


def per_device(sent_grad, gates, slot_token, slot_rank, pre_act, down_weight):
    rows_local = sent_grad[0]
    gate_local = gates[0]
    tokens = slot_token[0]
    ranks_here = slot_rank[0]
    weight = down_weight[0]
    saved_pre = pre_act[0]
    slot_count = tokens.shape[0]
    arrived = shifted(rows_local, "section", -1)
    start_sums = (
        jnp.zeros((slot_count, weight.shape[0]), jnp.float32),
        jnp.zeros((slot_count, 2), jnp.float32),
    )
    rows_piece = lax.all_gather(arrived, "blk", axis=0, tiled=True)
    gate_piece = lax.all_gather(gate_local, "blk", axis=0, tiled=True)
    piece_rows = rows_piece.shape[0]
    product = lax.dot_general(
        rows_piece, weight, (((1,), (1,)), ((), ())), preferred_element_type=jnp.float32
    )
    inside = (tokens >= 0) & (tokens < piece_rows)
    clipped = jnp.clip(tokens, 0, piece_rows - 1)
    rows_here = jnp.take(product, clipped, axis=0)
    gates_here = jnp.take(gate_piece, clipped, axis=0).astype(jnp.float32)
    summed_rows = jnp.where(inside[:, None], rows_here, start_sums[0])
    summed_gates = jnp.where(inside[:, None], gates_here, start_sums[1])
    weight_of = jnp.where(ranks_here == 0, summed_gates[:, 0], summed_gates[:, 1])
    gate_pre = saved_pre[:, 0, :].astype(jnp.float32)
    up_pre = saved_pre[:, 1, :].astype(jnp.float32)
    sigmoid_gate = jax.nn.sigmoid(gate_pre)
    activated = gate_pre * sigmoid_gate
    hidden = lax.optimization_barrier((activated * up_pre).astype(jnp.bfloat16)).astype(jnp.float32)
    partial_gate = jnp.sum(hidden * summed_rows, axis=1)
    grad_hidden = weight_of[:, None] * summed_rows
    d_up = grad_hidden * activated
    d_gp = grad_hidden * up_pre * sigmoid_gate * (1.0 + gate_pre * (1.0 - sigmoid_gate))
    d_pre = jnp.stack([d_gp, d_up], axis=1).astype(jnp.bfloat16)
    d_gate = lax.psum(partial_gate, "blk")
    return (d_pre[None], d_gate[None])


def solution(mesh):
    placed = (
        P("section", "blk", None),
        P("section", "blk", None),
        P("section", None),
        P("section", None),
        P("section", None, None, "blk"),
        P("section", "blk", None),
    )
    return jax.shard_map(
        per_device,
        mesh=mesh,
        in_specs=placed,
        out_specs=(P("section", None, None, "blk"), P("section", None)),
        check_vma=False,
    )
```

profile of v0, /device:TPU:8, one launch (start us, length us, event | category | flops | bytes accessed | tf_op | source)
XLA Modules:
  0.0 424.6 jit_solution(2917631482328893304)
XLA Ops:
  7.2 0.0 copy-start
  7.2 0.0 all-gather.3.cloned.1.call-start
  7.2 6.1 %collective-permute-start = (bf16[128,3072]{1,0:T(8,128)(2,1)}, bf16[128,3072]{1,0:T(8,128)(2,1)}, u32[]{:S(2)}, u32[]{:S(2)}) collective-permute-start(bf16[128,3072]{1,0:T(8,128)(2,1)} %bitcast.62), channel_id=1, source_target_pairs={{0,496},{16,0},{32,16},{48,32},{64,48},{80,64},{96,80},{112,96},{1... | collective-permute-start | bytes 2359304 | tf_op jit(solution)/shard_map/ppermute | solution.py:10
  13.4 9.8 %collective-permute-done = bf16[128,3072]{1,0:T(8,128)(2,1)} collective-permute-done((bf16[128,3072]{1,0:T(8,128)(2,1)}, bf16[128,3072]{1,0:T(8,128)(2,1)}, u32[]{:S(2)}, u32[]{:S(2)}) %collective-permute-start) | collective-permute-done | bytes 786464 | tf_op jit(solution)/shard_map/ppermute | solution.py:10
  23.2 0.0 all-gather.3.cloned.1.call-update
  23.2 0.7 compare_bitcast_fusion
  23.9 0.2 copy.12
  24.0 0.8 copy.11
  24.8 1.1 copy.16
  25.9 0.0 copy-start.1
  25.9 0.8 copy-done.1
  26.7 0.2 fusion.8
  26.9 89.3 %all-gather = bf16[1,2048,2]{2,1,0:T(8,128)(2,1)} all-gather(bf16[1,128,2]{2,1,0:T(8,128)(2,1)S(1)} %copy.11), channel_id=2, replica_groups=mesh['section'=32,'blk'=16] {'blk'}, dimensions={1}, use_global_device_ids=true | all-gather | bytes 8704 | tf_op jit(solution)/shard_map/all_gather | solution.py:27
  116.2 0.7 compare_select_fusion
  116.9 1.8 gather_fusion
  118.8 0.7 and_reduce_fusion
  119.5 0.7 broadcast_clamp_fusion
  120.2 0.1 convert_select_fusion
  120.3 0.2 fusion.22
  120.5 222.5 %all-gather.3.cloned.1.call-done = bf16[2048,3072]{1,0:T(8,128)(2,1)} async-done(((bf16[128,3072]{1,0:T(8,128)(2,1)}), bf16[2048,3072]{1,0:T(8,128)(2,1)}) %all-gather.3.cloned.1.call-update) | async-done | bytes 12582928 | tf_op jit(solution)/shard_map/all_gather | solution.py:26
  343.0 0.0 copy-done
  343.0 11.0 %fusion = f32[2048,512]{1,0:T(8,128)} fusion(bf16[2048,3072]{1,0:T(8,128)(2,1)} %all-gather.3.cloned.1.call-done, bf16[1,512,3072]{2,1,0:T(8,128)(2,1)S(1)} %copy-done), kind=kOutput, calls=%fused_computation.2 | convolution fusion | flops 6442450944 | bytes 19922944 | tf_op jit(solution)/shard_map/dot_general | solution.py:29
  354.0 4.2 gather_fusion.1
  358.2 1.5 fusion.21
  359.8 0.1 pad_maximum_fusion
  359.8 1.3 copy.14
  361.2 1.3 multiply_reduce_fusion
  362.4 55.4 %psum.7 = f32[1,256]{1,0:T(1,128)} all-reduce(f32[1,256]{1,0:T(1,128)S(1)} %bitcast.59), channel_id=1, replica_groups=mesh['section'=32,'blk'=16] {'blk'}, use_global_device_ids=true, to_apply=%region_1.2 | all-reduce | flops 256 | bytes 2048 | tf_op jit(solution)/shard_map/psum | solution.py:49
  (2 shorter events, 0.0 us)
Async XLA Ops:
  7.2 335.9 %copy-start = (bf16[1,512,3072]{2,1,0:T(8,128)(2,1)S(1)}, bf16[1,512,3072]{2,1,0:T(8,128)(2,1)}, u32[]{:S(2)}) copy-start(bf16[1,512,3072]{2,1,0:T(8,128)(2,1)} %param.11) | copy-start | bytes 9437188
  7.2 335.8 %all-gather.3.cloned.1.call-start = ((), (), s32[]{:S(2)}) async-start(), calls=%async_computation | async-start | bytes 13369344 | tf_op jit(solution)/shard_map/all_gather | solution.py:26
  7.2 15.9 %collective-permute-start = (bf16[128,3072]{1,0:T(8,128)(2,1)}, bf16[128,3072]{1,0:T(8,128)(2,1)}, u32[]{:S(2)}, u32[]{:S(2)}) collective-permute-start(bf16[128,3072]{1,0:T(8,128)(2,1)} %bitcast.62), channel_id=1, source_target_pairs={{0,496},{16,0},{32,16},{48,32},{64,48},{80,64},{96,80},{112,96},{1... | collective-permute-start | bytes 2359304 | tf_op jit(solution)/shard_map/ppermute | solution.py:10
  25.9 0.8 copy-start.1
Sparse Core Ops, SparseCore 0:
  23.3 319.6 all-gather.2
where the time goes:
time: 425 us
  waiting for transfers between devices  232 us (55%)
  blocking collectives  145 us (34%)
  between operations  14.1 us (3%)
  matrix products  11 us (3%)
  local copies, waits for them, and re-layouts  10.2 us (2%)
  starting transfers between devices  6.16 us (1%)
  other arithmetic  6.12 us (1%)
    all_gather x1, waiting for transfers between devices, per_device(): rows_piece = lax.all_gather(arrived, 'blk', axis=0, tiled=True)  223 us
    all_gather x1, blocking collectives, per_device(): gate_piece = lax.all_gather(gate_local, 'blk', axis=0, tiled=True)  89.3 us
    psum x1, blocking collectives, per_device(): d_gate = lax.psum(partial_gate, 'blk')  55.4 us
    dot_general x1, matrix products, per_device(): lax.dot_general(rows_piece, weight, (((1,), (1,)), ((), ())), preferred_e...  11 us
    ppermute x1, waiting for transfers between devices, shifted(): return lax.ppermute(value, axis, pairs)  9.8 us
  transfers between devices with their start and end apart: 2, of which 2 were waited for; matrix products, arithmetic and copies ran while one was open for 2% of the time, Pallas kernels for 0%

commit v1 on v0

v1 whole, which is shorter than its diff:
```python
import functools

import jax
import jax.numpy as jnp
from jax import lax
from jax.experimental import pallas as pl
from jax.experimental.pallas import tpu as pltpu
from jax.sharding import PartitionSpec as P

MESH = pl.DeviceIdType.MESH
F32, BF16 = jnp.float32, jnp.bfloat16
NB = 16
GROUPS = 8
CHUNKS = 2
OFFSETS = (0, 3, 1, 2)


def iota(shape, dim):
    return lax.broadcasted_iota(jnp.int32, shape, dim)


def onehot(mask):
    return jnp.where(mask, 1.0, 0.0)


def dot(a, b, dims):
    return lax.dot_general(a, b, (dims, ((), ())), preferred_element_type=F32)


NN = ((1,), (0,))
NT = ((1,), (1,))


def relay_kernel(
    sections,
    tok_ref, rank_ref, gates_ref, rows_hbm, pre_hbm, w_hbm,
    dpre_ref, dgate_ref,
    x_v, w_v, pre_v, tokp_v, sb_v, r_v, g_v, wp_v, dg_v, pf_v, act_v, dgp_v, hid_v, dh_v,
    cp_sem, tok_sem, wp_send, wp_recv, a2a_send, a2a_recv, ag_send, ag_recv, dg_send, dg_recv,
):
    slots = tok_ref.shape[1]
    shard, width = x_v.shape
    units = w_v.shape[0]
    gw = width // GROUPS
    per = slots // NB
    s, b = lax.axis_index("section"), lax.axis_index("blk")
    h, x = b // 4, lax.rem(b, 4)
    up, down = lax.rem(s + 1, sections), lax.rem(s + sections - 1, sections)

    def at(dx, dh):
        return lax.rem(h + dh, 4) * 4 + lax.rem(x + dx, 4)

    copies = [
        pltpu.make_async_copy(src, dst, cp_sem.at[i])
        for i, (src, dst) in enumerate(((rows_hbm, x_v), (pre_hbm, pre_v), (w_hbm, w_v)))
    ]
    for copy in copies:
        copy.start()

    barrier = pltpu.get_barrier_semaphore()

    def greet(section, index):
        pl.semaphore_signal(barrier, inc=1, device_id=(section, index), device_id_type=MESH)

    greet(down, b)
    for i in range(NB):
        greet(up, lax.rem(b + i, NB))
    for i in range(1, NB):
        greet(s, lax.rem(b + i, NB))
    pl.semaphore_wait(barrier, 2 * NB)

    tok_copy = pltpu.make_async_remote_copy(
        tok_ref, tokp_v, tok_sem.at[0], tok_sem.at[1], device_id=(up, b), device_id_type=MESH
    )
    tok_copy.start()

    tokens = tok_ref[...]
    block = tokens // shard
    q = iota((slots, slots), 0)
    r = iota((slots, slots), 1)
    source = q // NB
    start = jnp.sum(onehot(block < source), axis=1, keepdims=True).astype(jnp.int32)
    later = jnp.where(r - start >= NB, 1, 0)
    found = onehot((block == source) & (later == lax.rem(q, 2))).astype(BF16)
    p = iota((GROUPS * per, slots), 0)
    wanted = onehot(iota((GROUPS * per, slots), 1) == lax.rem(p, per) * NB + b).astype(BF16)
    pack = dot(wanted, found, NT)
    same = (iota(pack.shape, 0) // per) == lax.rem(iota(pack.shape, 1), NB) // 2
    pack = jnp.where(same, pack, 0.0).astype(BF16)

    copies[0].wait()
    tok_copy.wait()
    tokens_below = tokp_v[...]
    first = jnp.sum(onehot(tokens_below < b * shard), axis=1, keepdims=True).astype(jnp.int32)
    later_below = jnp.where(r - first >= NB, 1, 0)
    owner = onehot((lax.rem(r, NB) == q // NB) & (later_below == lax.rem(q, 2))).astype(BF16)
    t = iota((shard, slots), 0)
    where_token = onehot(tokens_below - b * shard == t).astype(BF16)
    select = dot(owner, where_token, NT)
    group = lax.rem(iota(select.shape, 0), NB) // 2
    picked = jnp.zeros((slots, gw), F32)
    for g in range(GROUPS):
        mine = jnp.where(group == g, select, 0.0).astype(BF16)
        picked += dot(mine, x_v[:, g * gw:(g + 1) * gw], NN)
    sb_v[...] = picked.astype(BF16)

    a2a = []
    for i in range(NB):
        to = lax.rem(b + i, NB)
        copy = pltpu.make_async_remote_copy(
            sb_v.at[pl.ds(pl.multiple_of(to * NB, NB), NB)],
            r_v.at[pl.ds(pl.multiple_of(b * NB, NB), NB)],
            a2a_send.at[i], a2a_recv.at[i], device_id=(down, to), device_id_type=MESH,
        )
        copy.start()
        a2a.append(copy)

    here = onehot(tokens - b * shard == t).astype(BF16)
    both = dot(gates_ref[...], here, NN)
    part = jnp.where(rank_ref[...] == 0, both[0:1, :], both[1:2, :])
    wp_v[b] = jnp.broadcast_to(part, (8, slots))

    def exchange(buffer, send, recv):
        started = []
        for i in range(1, NB):
            copy = pltpu.make_async_remote_copy(
                buffer.at[b], buffer.at[b], send.at[i], recv.at[i],
                device_id=(s, lax.rem(b + i, NB)), device_id_type=MESH,
            )
            copy.start()
            started.append(copy)
        return started

    weights = exchange(wp_v, wp_send, wp_recv)

    copies[1].wait()
    pf_v[...] = pre_v[...].astype(F32)
    tiles = units // 128
    stride = NB * 2 * tiles
    for o in range(NB):
        for c in range(tiles):
            gate = pf_v[pl.ds(2 * tiles * o + 2 * c, per, stride=stride), :]
            up_pre = pf_v[pl.ds(2 * tiles * o + 2 * c + 1, per, stride=stride), :]
            sig = jax.nn.sigmoid(gate)
            activated = gate * sig
            into = (pl.ds(o * per, per), pl.ds(c * 128, 128))
            act_v[into] = activated
            dgp_v[into] = up_pre * sig * (1.0 + gate * (1.0 - sig))
            hid_v[into] = (activated * up_pre).astype(BF16).astype(F32)

    for copy in a2a:
        copy.wait_recv()
    rows = GROUPS * per // CHUNKS
    started = {}

    def send(name, chunk, owner_blk, part, to):
        low, size = chunk * rows, rows
        if part is not None:
            size = rows // 2
            low += part * size
        index = list(NAMES).index(name)
        ref = g_v.at[owner_blk, pl.ds(low, size)]
        copy = pltpu.make_async_remote_copy(
            ref, ref, ag_send.at[chunk * len(NAMES) + index], ag_recv.at[chunk * len(NAMES) + index],
            device_id=(s, to), device_id_type=MESH,
        )
        copy.start()
        started[name, chunk] = copy

    def arrived(name, chunk):
        started[name, chunk].wait_recv()

    def x_send(i, c):
        send(f"x+{i}", c, at(0, OFFSETS[i]), None, at(1, 0))
        send(f"x-{i}", c, at(0, OFFSETS[i]), None, at(3, 0))

    def x_forward(i, c):
        arrived(f"x+{i}", c)
        send(f"xf+{i}", c, at(3, OFFSETS[i]), 0, at(1, 0))
        arrived(f"x-{i}", c)
        send(f"xf-{i}", c, at(1, OFFSETS[i]), 1, at(3, 0))

    def z_forward(c):
        arrived("z+", c)
        send("zf+", c, at(0, 3), 0, at(0, 1))
        arrived("z-", c)
        send("zf-", c, at(0, 1), 1, at(0, 3))
        x_send(1, c)
        x_send(2, c)

    def z_last(c):
        arrived("zf+", c)
        arrived("zf-", c)
        x_send(3, c)

    dh_v[...] = jnp.zeros_like(dh_v)

    def multiply(c):
        for i in range(4):
            arrived(f"xf+{i}", c)
            arrived(f"xf-{i}", c)
        for g in range(c * GROUPS // CHUNKS, (c + 1) * GROUPS // CHUNKS):
            left = g_v[:, g * per:(g + 1) * per, :].reshape(slots, gw)
            dh_v[...] += dot(left, w_v[:, g * gw:(g + 1) * gw], NT)

    for c in range(CHUNKS):
        g_v[b, c * rows:(c + 1) * rows] = dot(pack[c * rows:(c + 1) * rows], r_v[...], NN).astype(BF16)
        send("z+", c, b, None, at(0, 1))
        send("z-", c, b, None, at(0, 3))
        x_send(0, c)
    for c in range(CHUNKS):
        x_forward(0, c)
    for copy in weights:
        copy.wait()
    weight_row = jnp.sum(jnp.sum(wp_v[...], axis=0)[0:1], axis=0, keepdims=True)
    in_place = r == lax.rem(q, per) * NB + q // per
    weight = jnp.sum(jnp.where(in_place, weight_row, 0.0), axis=1, keepdims=True)
    copies[2].wait()
    for c in range(CHUNKS):
        z_forward(c)
        if c:
            x_forward(1, c - 1)
            x_forward(2, c - 1)
    z_last(0)
    x_forward(1, CHUNKS - 1)
    x_forward(2, CHUNKS - 1)
    for c in range(1, CHUNKS):
        z_last(c)
        x_forward(3, c - 1)
    multiply(0)
    x_forward(3, CHUNKS - 1)
    for c in range(1, CHUNKS):
        multiply(c)

    dh = dh_v[...]
    share = jnp.sum(hid_v[...] * dh, axis=1, keepdims=True)
    dg_v[b] = jnp.broadcast_to(jnp.sum(jnp.where(in_place, share, 0.0), axis=0, keepdims=True), (8, slots))
    sums = exchange(dg_v, dg_send, dg_recv)

    grad = weight * dh
    d_gate_pre = grad * dgp_v[...]
    d_up = grad * act_v[...]
    for o in range(NB):
        for c in range(tiles):
            part = (slice(o * per, (o + 1) * per), slice(c * 128, (c + 1) * 128))
            pf_v[pl.ds(2 * tiles * o + 2 * c, per, stride=stride), :] = d_gate_pre[part]
            pf_v[pl.ds(2 * tiles * o + 2 * c + 1, per, stride=stride), :] = d_up[part]
    dpre_ref[...] = pf_v[...].astype(BF16)

    for copy in sums:
        copy.wait()
    total = dg_v[0]
    for i in range(1, NB):
        total += dg_v[i]
    dgate_ref[...] = total[0:1]

    tok_copy_done = [*a2a, *started.values()]
    for copy in tok_copy_done:
        copy.wait_send()


NAMES = ("z+", "z-", "zf+", "zf-") + tuple(
    f"{kind}{i}" for i in range(4) for kind in ("x+", "x-", "xf+", "xf-")
)


def per_device(sections, sent_grad, gates, slot_token, slot_rank, pre_act, down_weight):
    rows, weight = sent_grad[0], down_weight[0]
    shard, width = rows.shape
    slots, _, units = pre_act.shape[1:]
    tiles = units // 128
    gw, per = width // GROUPS, slots // NB
    pre = pre_act[0].reshape(slots, 2, tiles, 128).transpose(0, 2, 1, 3).reshape(slots * tiles * 2, 128)
    vmem = pl.BlockSpec(memory_space=pltpu.VMEM)
    hbm = pl.BlockSpec(memory_space=pl.ANY)
    dma = pltpu.SemaphoreType.DMA
    n_ag = CHUNKS * len(NAMES)
    d_pre, d_gate = pl.pallas_call(
        functools.partial(relay_kernel, sections),
        out_shape=(
            jax.ShapeDtypeStruct(pre.shape, BF16),
            jax.ShapeDtypeStruct((1, slots), F32),
        ),
        in_specs=[vmem, vmem, vmem, hbm, hbm, hbm],
        out_specs=(vmem, vmem),
        scratch_shapes=[
            pltpu.VMEM((shard, width), BF16),
            pltpu.VMEM(weight.shape, BF16),
            pltpu.VMEM(pre.shape, BF16),
            pltpu.VMEM((1, slots), jnp.int32),
            pltpu.VMEM((slots, gw), BF16),
            pltpu.VMEM((slots, gw), BF16),
            pltpu.VMEM((NB, GROUPS * per, gw), BF16),
            pltpu.VMEM((NB, 8, slots), F32),
            pltpu.VMEM((NB, 8, slots), F32),
            pltpu.VMEM(pre.shape, F32),
            pltpu.VMEM((slots, units), F32),
            pltpu.VMEM((slots, units), F32),
            pltpu.VMEM((slots, units), F32),
            pltpu.VMEM((slots, units), F32),
            dma((3,)), dma((2,)), dma((NB,)), dma((NB,)), dma((NB,)), dma((NB,)),
            dma((n_ag,)), dma((n_ag,)), dma((NB,)), dma((NB,)),
        ],
        compiler_params=pltpu.CompilerParams(
            collective_id=0, has_side_effects=True, vmem_limit_bytes=56 * 2**20
        ),
    )(slot_token, slot_rank, gates[0].T, rows, pre, weight)
    d_pre = d_pre.reshape(slots, tiles, 2, 128).transpose(0, 2, 1, 3).reshape(1, slots, 2, units)
    return d_pre, d_gate


def solution(mesh):
    placed = (
        P("section", "blk", None),
        P("section", "blk", None),
        P("section", None),
        P("section", None),
        P("section", None, None, "blk"),
        P("section", "blk", None),
    )
    return jax.shard_map(
        functools.partial(per_device, mesh.shape["section"]),
        mesh=mesh,
        in_specs=placed,
        out_specs=(P("section", None, None, "blk"), P("section", None)),
        check_vma=False,
    )
```

time: 425 us -> 80.5 us (0.19)
  the two profiles are of different devices: /device:TPU:8 before, /device:TPU:6 now
where the time goes in v1:
time: 80.5 us; the launch traced here: 80.3 us
  Pallas kernels  76.3 us (95%)
  local copies, waits for them, and re-layouts  3.39 us (4%)
    pallas_call x1, Pallas kernels, per_device(): pl.pallas_call(functools.partial(relay_kernel, sections), out_shape=(jax....  76.3 us
    unnamed x2, local copies, waits for them, and re-layouts  3.39 us

profile of v1, /device:TPU:6, one launch (start us, length us, event | category | flops | bytes accessed | tf_op | source)
XLA Modules:
  0.0 80.3 jit_solution(10107297109864240534)
XLA Ops:
  0.6 76.3 %shard_map.77 = (bf16[2048,128]{1,0:T(8,128)(2,1)}, f32[1,256]{1,0:T(1,128)}) custom-call(s32[1,256]{1,0:T(1,128)} %tok_ref.1, s32[1,256]{1,0:T(1,128)} %rank_ref.1, bf16[2,128]{1,0:T(2,128)(2,1)} %bitcast.19, bf16[128,3072]{1,0:T(8,128)(2,1)} %bitcast.16, bf16[2048,128]{1,0:T(8,128)(2,1)} %bitcast.17, bf16[512,3072]{1,0:T(8,128)(2,1)} %bitcast.15), custom_call_target="tpu_custom_call" | custom-call | tf_op jit(solution)/shard_map/pallas_call | solution.py:278
  76.9 2.2 %copy.12 = bf16[1,256,2,512]{3,2,1,0:T(2,128)(2,1)} copy(bf16[1,256,2,512]{3,2,1,0:T(2,128)(2,1)} %bitcast.18) | data formatting | bytes 1048576
  79.1 1.2 %copy.13 = f32[1,256]{1,0:T(1,128)} copy(f32[1,256]{1,0:T(1,128)} %get-tuple-element.9) | data formatting | bytes 2048

commit v2 on v1

v2 whole, which is shorter than its diff:
```python
import functools

import jax
import jax.numpy as jnp
from jax import lax
from jax.experimental import pallas as pl
from jax.experimental.pallas import tpu as pltpu
from jax.sharding import PartitionSpec as P

MESH = pl.DeviceIdType.MESH
F32, BF16 = jnp.float32, jnp.bfloat16
NB = 16
GROUPS = 8
CHUNKS = 3
OFFSETS = (0, 3, 1, 2)


def iota(shape, dim):
    return lax.broadcasted_iota(jnp.int32, shape, dim)


def onehot(mask):
    return jnp.where(mask, 1.0, 0.0)


def dot(a, b, dims):
    return lax.dot_general(a, b, (dims, ((), ())), preferred_element_type=F32)


NN = ((1,), (0,))
NT = ((1,), (1,))


def relay_kernel(
    sections,
    tok_hbm, rank_hbm, gates_hbm, rows_hbm, pre_hbm, w_hbm,
    dpre_hbm, dgate_hbm,
    tok_v, rank_v, gates_v, dpre_v, dsum_v, x_v, w_v, pre_v, tokp_v, sb_v, r_v, g_v, wp_v, dg_v, pf_v, act_v, dgp_v, hid_v, dh_v,
    far_sem, cp_sem, tok_sem, wp_send, wp_recv, a2a_send, a2a_recv, ag_send, ag_recv, dg_send, dg_recv,
):
    slots = tok_v.shape[1]
    shard, width = x_v.shape
    units = w_v.shape[0]
    cw = width // CHUNKS
    gw = cw // GROUPS
    per = slots // NB
    s, b = lax.axis_index("section"), lax.axis_index("blk")
    h, x = b // 4, lax.rem(b, 4)
    up, down = lax.rem(s + 1, sections), lax.rem(s + sections - 1, sections)

    def at(dx, dh):
        return lax.rem(h + dh, 4) * 4 + lax.rem(x + dx, 4)

    everyone = [at(dx, dh) for dh in (2, 3, 1, 0) for dx in (2, 1, 3, 0)]

    barrier = pltpu.get_barrier_semaphore()

    def greet(section, index):
        pl.semaphore_signal(barrier, inc=1, device_id=(section, index), device_id_type=MESH)

    greet(down, b)
    for dh in (3, 1, 0):
        for dx in range(4):
            greet(up, at(dx, dh))
            if dx or dh:
                greet(s, at(dx, dh))

    def load(index, src, dst):
        copy = pltpu.make_async_copy(src, dst, cp_sem.at[index])
        copy.start()
        return copy

    small = [load(0, tok_hbm, tok_v), load(1, rank_hbm, rank_v), load(2, gates_hbm, gates_v)]
    got_rows = load(3, rows_hbm, x_v)
    got_pre = load(4, pre_hbm, pre_v)
    got_w = load(5, w_hbm, w_v)
    pl.semaphore_wait(barrier, 24)

    tok_copy = pltpu.make_async_remote_copy(
        tok_hbm, tokp_v, tok_sem.at[0], tok_sem.at[1], device_id=(up, b), device_id_type=MESH
    )
    tok_copy.start()
    pl.semaphore_signal(far_sem, inc=1, device_id=(s, at(0, 3)), device_id_type=MESH)
    for copy in small:
        copy.wait()

    tokens = tok_v[...]
    block = tokens // shard
    q = iota((slots, slots), 0)
    r = iota((slots, slots), 1)
    source = q // NB
    start = jnp.sum(onehot(block < source), axis=1, keepdims=True).astype(jnp.int32)
    later = jnp.where(r - start >= NB, 1, 0)
    found = onehot((block == source) & (later == lax.rem(q, 2))).astype(BF16)
    p = iota((GROUPS * per, slots), 0)
    wanted = onehot(iota((GROUPS * per, slots), 1) == lax.rem(p, per) * NB + b).astype(BF16)
    pack = dot(wanted, found, NT)
    same = (iota(pack.shape, 0) // per) == lax.rem(iota(pack.shape, 1), NB) // 2
    pack = jnp.where(same, pack, 0.0).astype(BF16)

    got_rows.wait()
    tok_copy.wait()
    tokens_below = tokp_v[...]
    first = jnp.sum(onehot(tokens_below < b * shard), axis=1, keepdims=True).astype(jnp.int32)
    later_below = jnp.where(r - first >= NB, 1, 0)
    owner = onehot((lax.rem(r, NB) == q // NB) & (later_below == lax.rem(q, 2))).astype(BF16)
    t = iota((shard, slots), 0)
    where_token = onehot(tokens_below - b * shard == t).astype(BF16)
    select = dot(owner, where_token, NT)
    group = lax.rem(iota(select.shape, 0), NB) // 2
    select = jnp.concatenate([jnp.where(group == g, select, 0.0).astype(BF16) for g in range(GROUPS)], axis=1)
    a2a = []
    for c in range(CHUNKS):
        low = c * cw
        stacked = jnp.concatenate([x_v[:, low + g * gw:low + (g + 1) * gw] for g in range(GROUPS)], axis=0)
        sb_v[c] = dot(select, stacked, NN).astype(BF16)
        if c == 0:
            pl.semaphore_wait(far_sem, 1)
        for i, to in enumerate(everyone):
            copy = pltpu.make_async_remote_copy(
                sb_v.at[c, pl.ds(pl.multiple_of(to * NB, NB), NB)],
                r_v.at[c, pl.ds(pl.multiple_of(b * NB, NB), NB)],
                a2a_send.at[c * NB + i], a2a_recv.at[c * NB + i], device_id=(down, to), device_id_type=MESH,
            )
            copy.start()
            a2a.append(copy)

    here = onehot(tokens - b * shard == t).astype(BF16)
    both = dot(gates_v[...], here, NN)
    part = jnp.where(rank_v[...] == 0, both[0:1, :], both[1:2, :])
    wp_v[b] = part

    def exchange(buffer, send, recv):
        started = []
        for i, to in enumerate(everyone[:-1]):
            copy = pltpu.make_async_remote_copy(
                buffer.at[b], buffer.at[b], send.at[i], recv.at[i], device_id=(s, to), device_id_type=MESH
            )
            copy.start()
            started.append(copy)
        return started

    weights = exchange(wp_v, wp_send, wp_recv)

    got_pre.wait()
    pf_v[...] = pre_v[...].astype(F32)
    tiles = units // 128
    stride = NB * 2 * tiles
    for o in range(NB):
        for c in range(tiles):
            gate = pf_v[pl.ds(2 * tiles * o + 2 * c, per, stride=stride), :]
            up_pre = pf_v[pl.ds(2 * tiles * o + 2 * c + 1, per, stride=stride), :]
            sig = jax.nn.sigmoid(gate)
            activated = gate * sig
            into = (pl.ds(o * per, per), pl.ds(c * 128, 128))
            act_v[into] = activated
            dgp_v[into] = up_pre * sig * (1.0 + gate * (1.0 - sig))
            hid_v[into] = (activated * up_pre).astype(BF16).astype(F32)

    rows = GROUPS * per
    started = {}

    def send(name, chunk, owner_blk, part, to):
        low, size = (0, rows) if part is None else (part * rows // 2, rows // 2)
        index = list(NAMES).index(name)
        ref = g_v.at[chunk, owner_blk, pl.ds(low, size)]
        copy = pltpu.make_async_remote_copy(
            ref, ref, ag_send.at[chunk * len(NAMES) + index], ag_recv.at[chunk * len(NAMES) + index],
            device_id=(s, to), device_id_type=MESH,
        )
        copy.start()
        started[name, chunk] = copy

    def arrived(name, chunk):
        started[name, chunk].wait_recv()

    def x_send(i, c):
        send(f"x+{i}", c, at(0, OFFSETS[i]), None, at(1, 0))
        send(f"x-{i}", c, at(0, OFFSETS[i]), None, at(3, 0))
        send(f"xo{i}", c, at(0, OFFSETS[i]), None, at(2, 0))

    def z_forward(c):
        arrived("z+", c)
        send("zf+", c, at(0, 3), 0, at(0, 1))
        arrived("z-", c)
        send("zf-", c, at(0, 1), 1, at(0, 3))
        x_send(1, c)
        x_send(2, c)

    def z_last(c):
        arrived("zf+", c)
        arrived("zf-", c)
        x_send(3, c)

    def multiply(c):
        for i in range(4):
            for kind in ("x+", "x-", "xo"):
                arrived(f"{kind}{i}", c)
        left = [g_v[c, :, g * per:(g + 1) * per, :].reshape(slots, gw) for g in range(GROUPS)]
        product = dot(jnp.concatenate(left, axis=1), w_v[:, c * cw:(c + 1) * cw], NT)
        dh_v[...] = product if c == 0 else dh_v[...] + product

    for c in range(CHUNKS):
        for copy in a2a[c * NB:(c + 1) * NB]:
            copy.wait_recv()
        g_v[c, b] = dot(pack, r_v[c], NN).astype(BF16)
        send("z+", c, b, None, at(0, 1))
        send("z-", c, b, None, at(0, 3))
        x_send(0, c)
    z_forward(0)
    for copy in weights:
        copy.wait()
    weight_row = jnp.sum(wp_v[...], axis=0)
    in_place = r == lax.rem(q, per) * NB + q // per
    weight = jnp.sum(jnp.where(in_place, weight_row, 0.0), axis=1, keepdims=True)
    got_w.wait()
    for c in range(1, CHUNKS):
        z_forward(c)
    for c in range(CHUNKS):
        z_last(c)
    for c in range(CHUNKS):
        multiply(c)

    dh = dh_v[...]
    share = jnp.sum(hid_v[...] * dh, axis=1, keepdims=True)
    dg_v[b] = jnp.sum(jnp.where(in_place, share, 0.0), axis=0, keepdims=True)
    sums = exchange(dg_v, dg_send, dg_recv)

    grad = weight * dh
    d_gate_pre = grad * dgp_v[...]
    d_up = grad * act_v[...]
    for o in range(NB):
        for c in range(tiles):
            part = (slice(o * per, (o + 1) * per), slice(c * 128, (c + 1) * 128))
            pf_v[pl.ds(2 * tiles * o + 2 * c, per, stride=stride), :] = d_gate_pre[part]
            pf_v[pl.ds(2 * tiles * o + 2 * c + 1, per, stride=stride), :] = d_up[part]
    dpre_v[...] = pf_v[...].astype(BF16)
    put_pre = load(0, dpre_v, dpre_hbm)

    for copy in sums:
        copy.wait()
    total = dg_v[0]
    for i in range(1, NB):
        total += dg_v[i]
    dsum_v[...] = total
    put_gate = load(1, dsum_v, dgate_hbm)

    for copy in [*a2a, *started.values()]:
        copy.wait_send()
    put_pre.wait()
    put_gate.wait()


def hand_on_kernel(dpre_ref, dgate_ref, dpre_out, dgate_out):
    dpre_out[...] = dpre_ref[...]
    dgate_out[...] = dgate_ref[...]


NAMES = ("z+", "z-", "zf+", "zf-") + tuple(f"{kind}{i}" for i in range(4) for kind in ("x+", "x-", "xo"))


def per_device(sections, sent_grad, gates, slot_token, slot_rank, pre_act, down_weight):
    rows, weight = sent_grad[0], down_weight[0]
    shard, width = rows.shape
    slots, _, units = pre_act.shape[1:]
    tiles = units // 128
    gw, per = width // CHUNKS // GROUPS, slots // NB
    pre = pre_act[0].reshape(slots, 2, tiles, 128).transpose(0, 2, 1, 3).reshape(slots * tiles * 2, 128)
    vmem = pl.BlockSpec(memory_space=pltpu.VMEM)
    hbm = pl.BlockSpec(memory_space=pl.ANY)
    dma = pltpu.SemaphoreType.DMA
    n_ag = CHUNKS * len(NAMES)
    d_pre, d_gate = pl.pallas_call(
        functools.partial(relay_kernel, sections),
        out_shape=(
            jax.ShapeDtypeStruct(pre.shape, BF16),
            jax.ShapeDtypeStruct((1, slots), F32),
        ),
        in_specs=[hbm] * 6,
        out_specs=(hbm, hbm),
        scratch_shapes=[
            pltpu.VMEM((1, slots), jnp.int32),
            pltpu.VMEM((1, slots), jnp.int32),
            pltpu.VMEM((2, shard), BF16),
            pltpu.VMEM(pre.shape, BF16),
            pltpu.VMEM((1, slots), F32),
            pltpu.VMEM((shard, width), BF16),
            pltpu.VMEM(weight.shape, BF16),
            pltpu.VMEM(pre.shape, BF16),
            pltpu.VMEM((1, slots), jnp.int32),
            pltpu.VMEM((CHUNKS, slots, gw), BF16),
            pltpu.VMEM((CHUNKS, slots, gw), BF16),
            pltpu.VMEM((CHUNKS, NB, GROUPS * per, gw), BF16),
            pltpu.VMEM((NB, 1, slots), F32),
            pltpu.VMEM((NB, 1, slots), F32),
            pltpu.VMEM(pre.shape, F32),
            pltpu.VMEM((slots, units), F32),
            pltpu.VMEM((slots, units), F32),
            pltpu.VMEM((slots, units), F32),
            pltpu.VMEM((slots, units), F32),
            pltpu.SemaphoreType.REGULAR, dma((6,)), dma((2,)), dma((NB,)), dma((NB,)), dma((CHUNKS * NB,)), dma((CHUNKS * NB,)),
            dma((n_ag,)), dma((n_ag,)), dma((NB,)), dma((NB,)),
        ],
        compiler_params=pltpu.CompilerParams(
            collective_id=0, has_side_effects=True, vmem_limit_bytes=56 * 2**20
        ),
    )(slot_token, slot_rank, gates[0].T, rows, pre, weight)
    d_pre, d_gate = pl.pallas_call(
        hand_on_kernel,
        out_shape=(
            jax.ShapeDtypeStruct(pre.shape, BF16),
            jax.ShapeDtypeStruct((1, slots), F32),
        ),
        in_specs=[vmem, vmem],
        out_specs=(vmem, vmem),
    )(d_pre, d_gate)
    d_pre = d_pre.reshape(slots, tiles, 2, 128).transpose(0, 2, 1, 3).reshape(1, slots, 2, units)
    return d_pre, d_gate


def solution(mesh):
    placed = (
        P("section", "blk", None),
        P("section", "blk", None),
        P("section", None),
        P("section", None),
        P("section", None, None, "blk"),
        P("section", "blk", None),
    )
    return jax.shard_map(
        functools.partial(per_device, mesh.shape["section"]),
        mesh=mesh,
        in_specs=placed,
        out_specs=(P("section", None, None, "blk"), P("section", None)),
        check_vma=False,
    )
```

time: 80.5 us -> 66.9 us (0.83)
  the two profiles are of different devices: /device:TPU:6 before, /device:TPU:2 now
where the time goes in v2:
time: 66.9 us; the launch traced here: 66.8 us
  Pallas kernels  66.2 us (99%)
    pallas_call x1, Pallas kernels, per_device(): pl.pallas_call(functools.partial(relay_kernel, sections), out_shape=(jax....  64.3 us
    pallas_call x1, Pallas kernels, per_device(): pl.pallas_call(hand_on_kernel, out_shape=(jax.ShapeDtypeStruct(pre.shape,...  1.87 us

profile of v2, /device:TPU:2, one launch (start us, length us, event | category | flops | bytes accessed | tf_op | source)
XLA Modules:
  0.0 66.8 jit_solution(16585661375191152116)
XLA Ops:
  0.6 64.3 %shard_map.77 = (bf16[2048,128]{1,0:T(8,128)(2,1)}, f32[1,256]{1,0:T(1,128)}) custom-call(s32[1,256]{1,0:T(1,128)} %tok_hbm.1, s32[1,256]{1,0:T(1,128)} %rank_hbm.1, bf16[2,128]{1,0:T(2,128)(2,1)} %bitcast.18, bf16[128,3072]{1,0:T(8,128)(2,1)} %bitcast.16, bf16[2048,128]{1,0:T(8,128)(2,1)} %bitcast.17, bf16[512,3072]{1,0:T(8,128)(2,1)} %bitcast.15), custom_call_target="tpu_custom_call" | custom-call | tf_op jit(solution)/shard_map/pallas_call | solution.py:273
  64.9 1.9 %shard_map.78 = (bf16[2048,128]{1,0:T(8,128)(2,1)}, f32[1,256]{1,0:T(1,128)}) custom-call(bf16[2048,128]{1,0:T(8,128)(2,1)} %get-tuple-element.6.dpre_ref, f32[1,256]{1,0:T(1,128)} %get-tuple-element.7.dgate_ref), custom_call_target="tpu_custom_call" | custom-call | tf_op jit(solution)/shard_map/pallas_call | solution.py:308

commit v3 on v2

--- a/solution.py
+++ b/solution.py
@@ -35,7 +35,7 @@
     sections,
     tok_hbm, rank_hbm, gates_hbm, rows_hbm, pre_hbm, w_hbm,
     dpre_hbm, dgate_hbm,
-    tok_v, rank_v, gates_v, dpre_v, dsum_v, x_v, w_v, pre_v, tokp_v, sb_v, r_v, g_v, wp_v, dg_v, pf_v, act_v, dgp_v, hid_v, dh_v,
+    place_v, tok_v, rank_v, gates_v, dpre_v, dsum_v, x_v, w_v, pre_v, tokp_v, sb_v, r_v, g_v, wp_v, dg_v, pf_v, act_v, dgp_v, hid_v, dh_v,
     far_sem, cp_sem, tok_sem, wp_send, wp_recv, a2a_send, a2a_recv, ag_send, ag_recv, dg_send, dg_recv,
 ):
     slots = tok_v.shape[1]
@@ -61,7 +61,6 @@
     greet(down, b)
     for dh in (3, 1, 0):
         for dx in range(4):
-            greet(up, at(dx, dh))
             if dx or dh:
                 greet(s, at(dx, dh))
 
@@ -74,20 +73,60 @@
     got_rows = load(3, rows_hbm, x_v)
     got_pre = load(4, pre_hbm, pre_v)
     got_w = load(5, w_hbm, w_v)
-    pl.semaphore_wait(barrier, 24)
+    pl.semaphore_wait(barrier, 12)
 
     tok_copy = pltpu.make_async_remote_copy(
         tok_hbm, tokp_v, tok_sem.at[0], tok_sem.at[1], device_id=(up, b), device_id_type=MESH
     )
     tok_copy.start()
+
+    got_rows.wait()
+    tok_copy.wait()
     pl.semaphore_signal(far_sem, inc=1, device_id=(s, at(0, 3)), device_id_type=MESH)
+    q = iota((slots, slots), 0)
+    r = iota((slots, slots), 1)
+    tokens_below = tokp_v[...]
+    first = jnp.sum(onehot(tokens_below < b * shard), axis=1, keepdims=True).astype(jnp.int32)
+    t = iota((shard, slots), 0)
+    where_token = onehot(tokens_below - b * shard == t).astype(BF16)
+    wide = iota((2 * NB, slots), 1)
+    line = iota((2 * NB, slots), 0)
+    later_below = jnp.where(wide - first >= NB, 1, 0)
+    owner = onehot((lax.rem(wide, NB) == lax.rem(line, NB)) & (later_below == line // NB)).astype(BF16)
+    select = dot(owner, where_token, NT).astype(BF16)
+    a2a = {}
+
+    def pick(c):
+        picked = dot(select, x_v[:, c * cw:(c + 1) * cw], NN)
+        for g in range(GROUPS):
+            for k in range(2):
+                place_v[pl.ds(2 * g + k, NB, stride=NB), :] = picked[k * NB:(k + 1) * NB, g * gw:(g + 1) * gw]
+        sb_v[c] = place_v[...].astype(BF16)
+
+    def deal(c, who):
+        for i in who:
+            to = everyone[i]
+            copy = pltpu.make_async_remote_copy(
+                sb_v.at[c, pl.ds(pl.multiple_of(to * NB, NB), NB)],
+                r_v.at[c, pl.ds(pl.multiple_of(b * NB, NB), NB)],
+                a2a_send.at[c * NB + i], a2a_recv.at[c * NB + i], device_id=(down, to), device_id_type=MESH,
+            )
+            copy.start()
+            a2a[c, i] = copy
+
+    far, near = range(4), range(4, NB)
+    pick(0)
+    for c in range(CHUNKS):
+        pick(c)
+        deal(c, near)
+    pl.semaphore_wait(far_sem, 1)
+    for c in range(CHUNKS):
+        deal(c, far)
+
     for copy in small:
         copy.wait()
-
     tokens = tok_v[...]
     block = tokens // shard
-    q = iota((slots, slots), 0)
-    r = iota((slots, slots), 1)
     source = q // NB
     start = jnp.sum(onehot(block < source), axis=1, keepdims=True).astype(jnp.int32)
     later = jnp.where(r - start >= NB, 1, 0)
@@ -97,33 +136,6 @@
     pack = dot(wanted, found, NT)
     same = (iota(pack.shape, 0) // per) == lax.rem(iota(pack.shape, 1), NB) // 2
     pack = jnp.where(same, pack, 0.0).astype(BF16)
-
-    got_rows.wait()
-    tok_copy.wait()
-    tokens_below = tokp_v[...]
-    first = jnp.sum(onehot(tokens_below < b * shard), axis=1, keepdims=True).astype(jnp.int32)
-    later_below = jnp.where(r - first >= NB, 1, 0)
-    owner = onehot((lax.rem(r, NB) == q // NB) & (later_below == lax.rem(q, 2))).astype(BF16)
-    t = iota((shard, slots), 0)
-    where_token = onehot(tokens_below - b * shard == t).astype(BF16)
-    select = dot(owner, where_token, NT)
-    group = lax.rem(iota(select.shape, 0), NB) // 2
-    select = jnp.concatenate([jnp.where(group == g, select, 0.0).astype(BF16) for g in range(GROUPS)], axis=1)
-    a2a = []
-    for c in range(CHUNKS):
-        low = c * cw
-        stacked = jnp.concatenate([x_v[:, low + g * gw:low + (g + 1) * gw] for g in range(GROUPS)], axis=0)
-        sb_v[c] = dot(select, stacked, NN).astype(BF16)
-        if c == 0:
-            pl.semaphore_wait(far_sem, 1)
-        for i, to in enumerate(everyone):
-            copy = pltpu.make_async_remote_copy(
-                sb_v.at[c, pl.ds(pl.multiple_of(to * NB, NB), NB)],
-                r_v.at[c, pl.ds(pl.multiple_of(b * NB, NB), NB)],
-                a2a_send.at[c * NB + i], a2a_recv.at[c * NB + i], device_id=(down, to), device_id_type=MESH,
-            )
-            copy.start()
-            a2a.append(copy)
 
     here = onehot(tokens - b * shard == t).astype(BF16)
     both = dot(gates_v[...], here, NN)
@@ -201,8 +213,8 @@
         dh_v[...] = product if c == 0 else dh_v[...] + product
 
     for c in range(CHUNKS):
-        for copy in a2a[c * NB:(c + 1) * NB]:
-            copy.wait_recv()
+        for i in range(NB):
+            a2a[c, i].wait_recv()
         g_v[c, b] = dot(pack, r_v[c], NN).astype(BF16)
         send("z+", c, b, None, at(0, 1))
         send("z-", c, b, None, at(0, 3))
@@ -245,7 +257,7 @@
     dsum_v[...] = total
     put_gate = load(1, dsum_v, dgate_hbm)
 
-    for copy in [*a2a, *started.values()]:
+    for copy in [*a2a.values(), *started.values()]:
         copy.wait_send()
     put_pre.wait()
     put_gate.wait()
@@ -279,6 +291,7 @@
         in_specs=[hbm] * 6,
         out_specs=(hbm, hbm),
         scratch_shapes=[
+            pltpu.VMEM((slots, gw), F32),
             pltpu.VMEM((1, slots), jnp.int32),
             pltpu.VMEM((1, slots), jnp.int32),
             pltpu.VMEM((2, shard), BF16),

time: 66.9 us -> 63.8 us (0.954)
  the two profiles are of different devices: /device:TPU:2 before, /device:TPU:32 now
where the time goes in v3:
time: 63.8 us; the launch traced here: 63.7 us
  Pallas kernels  63.1 us (99%)
  between operations  0.64 us (1%)
    pallas_call x1, Pallas kernels, per_device(): pl.pallas_call(functools.partial(relay_kernel, sections), out_shape=(jax....  61.2 us
    pallas_call x1, Pallas kernels, per_device(): pl.pallas_call(hand_on_kernel, out_shape=(jax.ShapeDtypeStruct(pre.shape,...  1.87 us

profile of v3, /device:TPU:32, one launch (start us, length us, event | category | flops | bytes accessed | tf_op | source)
XLA Modules:
  0.0 63.7 jit_solution(13418473199849738535)
XLA Ops:
  0.6 61.2 %shard_map.77 = (bf16[2048,128]{1,0:T(8,128)(2,1)}, f32[1,256]{1,0:T(1,128)}) custom-call(s32[1,256]{1,0:T(1,128)} %tok_hbm.1, s32[1,256]{1,0:T(1,128)} %rank_hbm.1, bf16[2,128]{1,0:T(2,128)(2,1)} %bitcast.18, bf16[128,3072]{1,0:T(8,128)(2,1)} %bitcast.16, bf16[2048,128]{1,0:T(8,128)(2,1)} %bitcast.17, bf16[512,3072]{1,0:T(8,128)(2,1)} %bitcast.15), custom_call_target="tpu_custom_call" | custom-call | tf_op jit(solution)/shard_map/pallas_call | solution.py:285
  61.8 1.9 %shard_map.78 = (bf16[2048,128]{1,0:T(8,128)(2,1)}, f32[1,256]{1,0:T(1,128)}) custom-call(bf16[2048,128]{1,0:T(8,128)(2,1)} %get-tuple-element.6.dpre_ref, f32[1,256]{1,0:T(1,128)} %get-tuple-element.7.dgate_ref), custom_call_target="tpu_custom_call" | custom-call | tf_op jit(solution)/shard_map/pallas_call | solution.py:321

commit v4 on v3

--- a/solution.py
+++ b/solution.py
@@ -187,9 +187,9 @@
         started[name, chunk].wait_recv()
 
     def x_send(i, c):
+        send(f"xo{i}", c, at(0, OFFSETS[i]), None, at(2, 0))
         send(f"x+{i}", c, at(0, OFFSETS[i]), None, at(1, 0))
         send(f"x-{i}", c, at(0, OFFSETS[i]), None, at(3, 0))
-        send(f"xo{i}", c, at(0, OFFSETS[i]), None, at(2, 0))
 
     def z_forward(c):
         arrived("z+", c)

time: 63.8 us -> 63.5 us (level)
  no operation moved by 1% of the time
where the time goes in v4:
time: 63.5 us; the launch traced here: 63.4 us
  Pallas kernels  62.7 us (99%)
  between operations  0.64 us (1%)
    pallas_call x1, Pallas kernels, per_device(): pl.pallas_call(functools.partial(relay_kernel, sections), out_shape=(jax....  60.8 us
    pallas_call x1, Pallas kernels, per_device(): pl.pallas_call(hand_on_kernel, out_shape=(jax.ShapeDtypeStruct(pre.shape,...  1.87 us

profile of v4, /device:TPU:32, one launch (start us, length us, event | category | flops | bytes accessed | tf_op | source)
XLA Modules:
  0.0 63.4 jit_solution(2002980361947822300)
XLA Ops:
  0.6 60.8 %shard_map.77 = (bf16[2048,128]{1,0:T(8,128)(2,1)}, f32[1,256]{1,0:T(1,128)}) custom-call(s32[1,256]{1,0:T(1,128)} %tok_hbm.1, s32[1,256]{1,0:T(1,128)} %rank_hbm.1, bf16[2,128]{1,0:T(2,128)(2,1)} %bitcast.18, bf16[128,3072]{1,0:T(8,128)(2,1)} %bitcast.16, bf16[2048,128]{1,0:T(8,128)(2,1)} %bitcast.17, bf16[512,3072]{1,0:T(8,128)(2,1)} %bitcast.15), custom_call_target="tpu_custom_call" | custom-call | tf_op jit(solution)/shard_map/pallas_call | solution.py:285
  61.5 1.9 %shard_map.78 = (bf16[2048,128]{1,0:T(8,128)(2,1)}, f32[1,256]{1,0:T(1,128)}) custom-call(bf16[2048,128]{1,0:T(8,128)(2,1)} %get-tuple-element.6.dpre_ref, f32[1,256]{1,0:T(1,128)} %get-tuple-element.7.dgate_ref), custom_call_target="tpu_custom_call" | custom-call | tf_op jit(solution)/shard_map/pallas_call | solution.py:321
